TPU v7x, 32 devices: a whole 2x2x4 slice. The times are simulated.
32 devices in a mesh: node: 8 (over y, x, core), local: 4 (over z).
Axes of the slice: x: 2, y: 2, z: 4, core: 2. Of those that a mesh axis runs over, the one named last changes fastest.
Arguments:
- quantized: bfloat16 [512, 3584], P(('node', 'local')), may hold values from -6 to 6
- scales: bfloat16 [512, 28], P(('node', 'local')), may hold values from 0.29882812 to 3
- expert_ids: int32 [512, 8], P(('node', 'local')), may hold values from 0 to 31, as said below
- node_choice: int32 [512, 4], P(('node', 'local')), may hold values from 0 to 7, as said below
- gate_weights: bfloat16 [512, 8], P(('node', 'local')), may hold values from 0.099609375 to 1
- w_gate: bfloat16 [32, 3584, 1024], P(('node', 'local')), may hold values from -0.09375 to 0.09375
- w_up: bfloat16 [32, 3584, 1024], P(('node', 'local')), may hold values from -0.09375 to 0.09375
- w_down: bfloat16 [32, 1024, 3584], P(('node', 'local')), may hold values from -0.1875 to 0.1875
Outputs:
- mixed: bfloat16 [512, 3584], P(('node', 'local'))
Inputs may be any that keep to these rules, and one draw needn't show every extreme that they name: `expert_ids`: each token names 8 distinct experts, all on nodes listed for it in node_choice (expert e is on node e // 4), and each listed node holds at least one of them. In every draw one expert is named exactly 8 times by the tokens of every device. `node_choice`: each token lists 4 distinct nodes. The tokens of one device (aligned blocks of 16 rows) list every node exactly 8 times, so they name each expert at most 8 times.
All inputs are finite; a program needn't handle non-finite values.
Results may differ from a plain program's by a relative error of at most 0.012.
Values may be sent and summed in bfloat16 or wider, within the bound.
A program may use at most 128 MiB of HBM per device.

v0:
```python
import jax
import jax.numpy as jnp
from jax import lax
from jax.sharding import PartitionSpec as P


def expert_apply(quant_rows, scale_rows, gate_proj, up_proj, down_proj):
    row_count = quant_rows.shape[0]
    blocks = scale_rows.shape[1]
    widened = (
        quant_rows.reshape(row_count, blocks, -1).astype(jnp.float32)
        * scale_rows.astype(jnp.float32)[:, :, None]
    )
    inputs = widened.reshape(row_count, -1).astype(jnp.bfloat16)
    gate_act = jnp.dot(inputs, gate_proj, preferred_element_type=jnp.float32)
    up_act = jnp.dot(inputs, up_proj, preferred_element_type=jnp.float32)
    hidden = (jax.nn.silu(gate_act) * up_act).astype(jnp.bfloat16)
    return jnp.dot(hidden, down_proj, preferred_element_type=jnp.float32).astype(jnp.bfloat16)


def place_matrix(target, slot_count):
    marked = (target[:, :, None] == jnp.arange(slot_count, dtype=jnp.int32)).any(axis=1)
    return marked.T.astype(jnp.bfloat16)


def place_rows(placing, values):
    return jnp.dot(placing, values, preferred_element_type=jnp.float32).astype(jnp.bfloat16)


def exclusive_rank(member_counts):
    return jnp.cumsum(member_counts, axis=0) - member_counts


def node_totals(partial_value):
    return jnp.sum(partial_value.astype(jnp.float32), axis=1).astype(jnp.bfloat16)


def shards(quantized, scales, expert_ids, node_choice, gate_weights, w_gate, w_up, w_down):
    n_node = lax.axis_size("node")
    n_local = lax.axis_size("local")
    experts = n_node * n_local
    tok_count = quantized.shape[0]
    model_width = quantized.shape[1]
    node_limit = node_choice.shape[1]
    capacity = node_limit * tok_count // n_node
    gate_proj = w_gate[0]
    up_proj = w_up[0]
    down_proj = w_down[0]
    node_of = expert_ids // n_local
    member = node_of[:, None, :] == node_choice[:, :, None]
    named = (
        (expert_ids[:, :, None] == jnp.arange(experts, dtype=jnp.int32))
        .any(axis=1)
        .astype(jnp.int32)
    )
    earlier = exclusive_rank(named)
    slot_index = jnp.take_along_axis(earlier, expert_ids, axis=1)
    target = expert_ids * capacity + slot_index
    placing = place_matrix(target, experts * capacity)
    send_quant = place_rows(placing, quantized).reshape(experts, capacity, model_width)
    send_scale = place_rows(placing, scales).reshape(experts, capacity, -1)
    quant_in = lax.all_to_all(
        send_quant, ("node", "local"), split_axis=0, concat_axis=0, tiled=True
    )
    scale_in = lax.all_to_all(
        send_scale, ("node", "local"), split_axis=0, concat_axis=0, tiled=True
    )
    senders = quant_in.shape[0]
    slots_in = quant_in.shape[1]
    result = expert_apply(
        quant_in.reshape(senders * slots_in, model_width),
        scale_in.reshape(senders * slots_in, -1),
        gate_proj,
        up_proj,
        down_proj,
    )
    returned = lax.all_to_all(
        result.reshape(senders, slots_in, model_width),
        ("node", "local"),
        split_axis=0,
        concat_axis=0,
        tiled=True,
    )
    picked = returned.reshape(experts * capacity, model_width)[target]
    weighted = (gate_weights.astype(jnp.float32)[:, :, None] * picked.astype(jnp.float32)).astype(
        jnp.bfloat16
    )
    partial_value = jnp.einsum(
        "tjk,tkd->tjd", member.astype(jnp.bfloat16), weighted, preferred_element_type=jnp.float32
    ).astype(jnp.bfloat16)
    return node_totals(partial_value)


def solution(mesh):
    return jax.shard_map(
        shards,
        mesh=mesh,
        in_specs=(
            P(("node", "local"), None),
            P(("node", "local"), None),
            P(("node", "local"), None),
            P(("node", "local"), None),
            P(("node", "local"), None),
            P(("node", "local"), None, None),
            P(("node", "local"), None, None),
            P(("node", "local"), None, None),
        ),
        out_specs=P(("node", "local"), None),
        check_vma=False,
    )
```

profile of v0, /device:TPU:1, one launch (start us, length us, event | category | flops | bytes accessed | tf_op | source)
XLA Modules:
  0.0 138.0 jit_solution(13128457790840069380)
XLA Ops:
  0.0 0.8 copy.31
  0.8 0.7 bitcast_or_fusion
  1.5 0.1 fusion.28
  1.7 0.1 reshape.76
  1.8 1.3 gather_fusion.1
  3.4 0.1 fusion.27
  3.5 0.2 convolution_convert_fusion.2
  3.7 0.7 copy.35
  4.4 7.1 %all-to-all-start.1 = ((bf16[32,8,28]{2,1,0:T(8,128)(2,1)}), bf16[32,8,28]{2,1,0:T(8,128)(2,1)S(1)}, u32[]{:S(2)}, u32[]{:S(2)}) async-start(bf16[32,8,28]{2,1,0:T(8,128)(2,1)} %bitcast.2), calls=%async_computation.1 | async-start | bytes 131072 | tf_op jit(solution)/shard_map/all_to_all | solution.py:65
  11.5 1.9 %fusion.9 = bf16[32,8,3584]{2,1,0:T(8,128)(2,1)} fusion(pred[16,256]{1,0:T(8,128)(4,1)S(1)} %fusion.27, bf16[16,3584]{1,0:T(8,128)(2,1)S(1)} %copy-done), kind=kOutput, calls=%fused_computation.10 | convolution fusion | flops 30277632 | bytes 1953792 | tf_op jit(solution)/shard_map/dot_general | solution.py:27
  13.5 4.9 %all-to-all-done.1 = bf16[32,8,28]{2,1,0:T(8,128)(2,1)S(1)} async-done(((bf16[32,8,28]{2,1,0:T(8,128)(2,1)}), bf16[32,8,28]{2,1,0:T(8,128)(2,1)S(1)}, u32[]{:S(2)}, u32[]{:S(2)}) %all-to-all-start.1) | async-done | bytes 14368 | tf_op jit(solution)/shard_map/all_to_all | solution.py:65
  18.4 3.2 %all-to-all-start = ((bf16[32,8,3584]{2,1,0:T(8,128)(2,1)}), bf16[32,8,3584]{2,1,0:T(8,128)(2,1)S(1)}, u32[]{:S(2)}, u32[]{:S(2)}) async-start(bf16[32,8,3584]{2,1,0:T(8,128)(2,1)} %fusion.9), calls=%async_computation | async-start | bytes 3670016 | tf_op jit(solution)/shard_map/all_to_all | solution.py:62
  21.6 42.9 %all-to-all-done = bf16[32,8,3584]{2,1,0:T(8,128)(2,1)S(1)} async-done(((bf16[32,8,3584]{2,1,0:T(8,128)(2,1)}), bf16[32,8,3584]{2,1,0:T(8,128)(2,1)S(1)}, u32[]{:S(2)}, u32[]{:S(2)}) %all-to-all-start) | async-done | bytes 1835040 | tf_op jit(solution)/shard_map/all_to_all | solution.py:62
  64.5 2.4 %reshape.66 = f32[256,28,128]{2,1,0:T(8,128)} reshape(bf16[32,8,3584]{2,1,0:T(8,128)(2,1)S(1)} %all-to-all-done) | data formatting | bytes 5505024 | tf_op jit(solution)/shard_map/convert_element_type | solution.py:11
  66.9 3.8 %multiply_convert_fusion = bf16[256,28,128]{2,1,0:T(8,128)(2,1)} fusion(f32[256,28,128]{2,1,0:T(8,128)} %reshape.66, f32[256,28]{1,0:T(8,128)S(1)} %bitcast_convert_fusion), kind=kLoop, calls=%fused_computation.13 | loop fusion | flops 1835008 | bytes 5533696 | tf_op jit(solution)/shard_map/convert_element_type | solution.py:14
  70.8 3.1 %copy.36 = bf16[256,28,128]{0,2,1:T(8,128)(2,1)S(1)} copy(bf16[256,28,128]{2,1,0:T(8,128)(2,1)} %multiply_convert_fusion) | data formatting | bytes 3670016 | tf_op jit(solution)/shard_map/convert_element_type | solution.py:14
  73.9 5.2 %fusion.4 = f32[256,1024]{1,0:T(8,128)S(1)} fusion(bf16[256,3584]{0,1:T(8,128)(2,1)S(1)} %bitcast.46, bf16[1,3584,1024]{2,1,0:T(8,128)(2,1)} %param.13), kind=kOutput, calls=%fused_computation.6 | convolution fusion | flops 1879048192 | bytes 10223616 | tf_op jit(solution)/shard_map/dot_general | solution.py:15
  79.1 10.5 %fusion.10 = bf16[32,8,3584]{2,1,0:T(8,128)(2,1)} fusion(bf16[1,1024,3584]{2,1,0:T(8,128)(2,1)} %param.15, bf16[256,3584]{0,1:T(8,128)(2,1)S(1)} %bitcast.47, bf16[1,3584,1024]{2,1,0:T(8,128)(2,1)} %param.14, f32[256,1024]{1,0:T(8,128)S(1)} %fusion.4), kind=kOutput, calls=%fused_computation.11 | convolution fusion | flops 3760586752 | bytes 19398656 | tf_op jit(solution)/shard_map/dot_general | solution.py:18
  89.5 3.1 %all-to-all-start.2 = ((bf16[32,8,3584]{2,1,0:T(8,128)(2,1)}), bf16[32,8,3584]{2,1,0:T(8,128)(2,1)S(1)}, u32[]{:S(2)}, u32[]{:S(2)}) async-start(bf16[32,8,3584]{2,1,0:T(8,128)(2,1)} %fusion.10), calls=%async_computation.2 | async-start | bytes 3670016 | tf_op jit(solution)/shard_map/all_to_all | solution.py:77
  92.7 0.1 reshape.70
  92.9 0.1 copy.29
  93.1 42.4 %all-to-all-done.2 = bf16[32,8,3584]{2,1,0:T(8,128)(2,1)S(1)} async-done(((bf16[32,8,3584]{2,1,0:T(8,128)(2,1)}), bf16[32,8,3584]{2,1,0:T(8,128)(2,1)S(1)}, u32[]{:S(2)}, u32[]{:S(2)}) %all-to-all-start.2) | async-done | bytes 1835040 | tf_op jit(solution)/shard_map/all_to_all | solution.py:77
  135.5 1.1 gather_fusion
  136.6 1.4 %fusion.20 = bf16[16,3584]{1,0:T(8,128)(2,1)} fusion(bf16[128,3584]{1,0:T(8,128)(2,1)S(1)} %gather_fusion, f32[16,8]{1,0:T(8,128)S(1)} %copy.30, s32[16,4]{1,0:T(8,128)S(1)} %copy.29, s32[16,8]{1,0:T(8,128)S(1)} %copy.28), kind=kOutput, calls=%fused_computation.18 | convolution fusion | flops 5448192 | bytes 1033472 | tf_op jit(solution)/shard_map/tjk,tkd->tjd/dot_general | solution.py:88
  (23 shorter events, 0.6 us)
Async XLA Ops:
  0.0 11.5 %copy-start = (bf16[16,3584]{1,0:T(8,128)(2,1)S(1)}, bf16[16,3584]{1,0:T(8,128)(2,1)}, u32[]{:S(2)}) copy-start(bf16[16,3584]{1,0:T(8,128)(2,1)} %param.8) | copy-start | bytes 344068
  1.8 1.5 %copy-start.1 = (s32[16,8]{0,1:T(8,128)S(1)}, s32[16,8]{0,1:T(8,128)}, u32[]{:S(2)}) copy-start(s32[16,8]{0,1:T(8,128)} %param.10) | copy-start | bytes 1540
  1.8 1.7 %copy-start.4 = (bf16[16,28]{1,0:T(8,128)(2,1)S(1)}, bf16[16,28]{1,0:T(8,128)(2,1)}, u32[]{:S(2)}) copy-start(bf16[16,28]{1,0:T(8,128)(2,1)} %param.9) | copy-start | bytes 2692
  4.4 13.9 %all-to-all-start.1 = ((bf16[32,8,28]{2,1,0:T(8,128)(2,1)}), bf16[32,8,28]{2,1,0:T(8,128)(2,1)S(1)}, u32[]{:S(2)}, u32[]{:S(2)}) async-start(bf16[32,8,28]{2,1,0:T(8,128)(2,1)} %bitcast.2), calls=%async_computation.1 | async-start | bytes 131072 | tf_op jit(solution)/shard_map/all_to_all | solution.py:65
  18.4 46.2 %all-to-all-start = ((bf16[32,8,3584]{2,1,0:T(8,128)(2,1)}), bf16[32,8,3584]{2,1,0:T(8,128)(2,1)S(1)}, u32[]{:S(2)}, u32[]{:S(2)}) async-start(bf16[32,8,3584]{2,1,0:T(8,128)(2,1)} %fusion.9), calls=%async_computation | async-start | bytes 3670016 | tf_op jit(solution)/shard_map/all_to_all | solution.py:62
  89.5 3.4 %copy-start.2 = (s32[16,4]{0,1:T(4,128)S(1)}, s32[16,4]{0,1:T(4,128)}, u32[]{:S(2)}) copy-start(s32[16,4]{0,1:T(4,128)} %param.11) | copy-start | bytes 772
  89.5 3.4 %copy-start.3 = (bf16[16,8]{0,1:T(8,128)(2,1)S(1)}, bf16[16,8]{0,1:T(8,128)(2,1)}, u32[]{:S(2)}) copy-start(bf16[16,8]{0,1:T(8,128)(2,1)} %param.12) | copy-start | bytes 772
  89.5 45.9 %all-to-all-start.2 = ((bf16[32,8,3584]{2,1,0:T(8,128)(2,1)}), bf16[32,8,3584]{2,1,0:T(8,128)(2,1)S(1)}, u32[]{:S(2)}, u32[]{:S(2)}) async-start(bf16[32,8,3584]{2,1,0:T(8,128)(2,1)} %fusion.10), calls=%async_computation.2 | async-start | bytes 3670016 | tf_op jit(solution)/shard_map/all_to_all | solution.py:77
where the time goes:
time: 138 us
  waiting for transfers between devices  90.2 us (65%)
  matrix products  19.2 us (14%)
  starting transfers between devices  13.4 us (10%)
  local copies, waits for them, and re-layouts  10.2 us (7%)
  other arithmetic  4.84 us (4%)
    all_to_all x1, waiting for transfers between devices, shards(): lax.all_to_all(send_quant, ('node', 'local'), split_axis=0, concat_axis=0...  42.9 us
    all_to_all x1, waiting for transfers between devices, shards(): lax.all_to_all(result.reshape(senders, slots_in, model_width), ('node', '...  42.4 us
    dot_general x1, matrix products, expert_apply(): jnp.dot(hidden, down_proj, preferred_element_type=jnp.float32)  10.5 us
    all_to_all x1, starting transfers between devices, shards(): lax.all_to_all(send_scale, ('node', 'local'), split_axis=0, concat_axis=0...  7.1 us
    dot_general x1, matrix products, expert_apply(): gate_act = jnp.dot(inputs, gate_proj, preferred_element_type=jnp.float32)  5.17 us
    all_to_all x1, waiting for transfers between devices, shards(): lax.all_to_all(send_scale, ('node', 'local'), split_axis=0, concat_axis=0...  4.89 us
    convert_element_type x1, other arithmetic, expert_apply(): inputs = widened.reshape(row_count, -1).astype(jnp.bfloat16)  3.84 us
    all_to_all x1, starting transfers between devices, shards(): lax.all_to_all(send_quant, ('node', 'local'), split_axis=0, concat_axis=0...  3.22 us
  transfers between devices with their start and end apart: 3, of which 3 were waited for; matrix products, arithmetic and copies ran while one was open for 2% of the time, Pallas kernels for 0%

commit v1 on v0

v1 whole, which is shorter than its diff:
```python
import functools
import jax
import jax.numpy as jnp
from jax import lax
from jax.experimental import pallas as pl
from jax.experimental.pallas import tpu as pltpu
from jax.sharding import PartitionSpec as P

MESH = pl.DeviceIdType.MESH
LANES = 128
F32 = jnp.float32
BF16 = jnp.bfloat16


def round_up(value, step):
    return (value + step - 1) // step * step


def kernel(
    n_node, n_local, cap, parts,
    q_ref, scale_ref, ids_ref, choice_ref, gate_ref, wg_hbm, wu_hbm, wd_hbm,
    out_ref,
    wg, wu, wd, xz, packed, rows, inputs, hidden, result, back, zpart, zback,
    w_sem, z_send, z_recv, n_send, n_recv, r_send, r_recv, t_send, t_recv,
):
    me_n = lax.axis_index("node")
    me_l = lax.axis_index("local")
    tok, width = q_ref.shape
    slots = n_node * cap
    total = n_local * slots
    exp_w = rows.shape[3] - width
    part_w = width // parts
    ff = wg.shape[1]

    def node_at(step):
        return lax.rem(me_n + step, n_node)

    def local_at(step):
        return lax.rem(me_l + step, n_local)

    weight_copies = [
        pltpu.make_async_copy(src, dst, w_sem.at[i])
        for i, (src, dst) in enumerate(((wg_hbm, wg), (wu_hbm, wu), (wd_hbm, wd)))
    ]
    barrier = pltpu.get_barrier_semaphore()
    for step in range(1, n_node):
        pl.semaphore_signal(barrier, inc=1, device_id=(node_at(step), me_l), device_id_type=MESH)
    for step in range(1, n_local):
        pl.semaphore_signal(barrier, inc=1, device_id=(me_n, local_at(step)), device_id_type=MESH)
    for copy in weight_copies:
        copy.start()

    scale = scale_ref[...].astype(F32)
    block = width // scale.shape[1]
    for b in range(scale.shape[1]):
        cols = pl.ds(b * block, block)
        xz[me_l, :, cols] = (q_ref[:, cols].astype(F32) * scale[:, b : b + 1]).astype(BF16)
    ids = ids_ref[...]
    gate = gate_ref[...].astype(F32)
    expert_col = lax.broadcasted_iota(jnp.int32, (tok, exp_w), 1)
    weight = jnp.zeros((tok, exp_w), F32)
    for k in range(ids.shape[1]):
        weight = weight + jnp.where(ids[:, k : k + 1] == expert_col, gate[:, k : k + 1], 0.0)
    xz[me_l, :, pl.ds(width, exp_w)] = weight.astype(BF16)
    place_w = xz.shape[2] - width - exp_w
    column = lax.broadcasted_iota(jnp.int32, (tok, place_w), 1)
    node_col = lax.div(column, jnp.int32(cap))
    slot_col = lax.rem(column, jnp.int32(cap))
    choice = choice_ref[...]
    named = jnp.zeros((tok, place_w), F32)
    for j in range(choice.shape[1]):
        named = named + jnp.where(choice[:, j : j + 1] == node_col, 1.0, 0.0)
    before = jnp.where(
        lax.broadcasted_iota(jnp.int32, (tok, tok), 1) < lax.broadcasted_iota(jnp.int32, (tok, tok), 0), 1.0, 0.0
    )
    rank = jnp.dot(before.astype(BF16), named.astype(BF16), preferred_element_type=F32)
    place = jnp.where(rank == slot_col.astype(F32), named, 0.0)
    xz[me_l, :, pl.ds(width + exp_w, place_w)] = place.astype(BF16)

    pl.semaphore_wait(barrier, n_node + n_local - 2)

    def z_copy(step):
        return pltpu.make_async_remote_copy(
            src_ref=xz.at[me_l], dst_ref=xz.at[me_l],
            send_sem=z_send.at[step], recv_sem=z_recv.at[step],
            device_id=(me_n, local_at(step)), device_id_type=MESH,
        )

    for step in range(1, n_local):
        z_copy(step).start()

    def n_copy(source, step):
        return pltpu.make_async_remote_copy(
            src_ref=packed.at[source, node_at(step)], dst_ref=rows.at[source, me_n],
            send_sem=n_send.at[source, step], recv_sem=n_recv.at[source, step],
            device_id=(node_at(step), me_l), device_id_type=MESH,
        )

    def pack(source):
        picks = jnp.transpose(xz[source, :, pl.ds(width + exp_w, place_w)].astype(F32))[:slots].astype(BF16)
        value = jnp.dot(picks, xz[source, :, pl.ds(0, width + exp_w)], preferred_element_type=F32)
        packed[source] = value.reshape(n_node, cap, width + exp_w).astype(BF16)

        @pl.loop(1, n_node)
        def _(step):
            n_copy(source, step).start()

        rows[source, me_n] = packed[source, me_n]

    pack(me_l)

    @pl.loop(1, n_local)
    def _(step):
        z_copy(step).wait_recv()
        pack(lax.rem(me_l - step + n_local, n_local))

    @pl.loop(0, n_local)
    def _(source):
        @pl.loop(1, n_node)
        def _(step):
            n_copy(source, step).wait_recv()

    inputs[...] = rows[:, :, :, :width].astype(F32).reshape(total, width).astype(BF16)
    weights = rows[:, :, :, width:].astype(F32).reshape(total, exp_w)
    mine = lax.broadcasted_iota(jnp.int32, (total, exp_w), 1) == me_n * n_local + me_l
    row_weight = jnp.sum(jnp.where(mine, weights, 0.0), axis=1, keepdims=True)
    weight_copies[0].wait()
    weight_copies[1].wait()
    tile = 256

    @pl.loop(0, ff // tile)
    def _(i):
        cols = pl.ds(pl.multiple_of(i * tile, tile), tile)
        g = jnp.dot(inputs[...], wg[:, cols], preferred_element_type=F32)
        u = jnp.dot(inputs[...], wu[:, cols], preferred_element_type=F32)
        hidden[:, cols] = (g / (1.0 + jnp.exp(-g)) * u).astype(BF16)

    weight_copies[2].wait()

    def r_copy(h, step):
        return pltpu.make_async_remote_copy(
            src_ref=result.at[h, :, node_at(step)], dst_ref=back.at[h, :, me_n],
            send_sem=r_send.at[h, step], recv_sem=r_recv.at[h, step],
            device_id=(node_at(step), me_l), device_id_type=MESH,
        )

    @pl.loop(0, parts)
    def _(h):
        cols = pl.ds(pl.multiple_of(h * part_w, LANES), part_w)
        y = jnp.dot(hidden[...], wd[:, cols], preferred_element_type=F32)
        y = row_weight * y.astype(BF16).astype(F32)
        result[h] = y.reshape(n_local, n_node, cap, part_w).astype(BF16)

        @pl.loop(1, n_node)
        def _(step):
            r_copy(h, step).start()

        back[h, :, me_n] = result[h, :, me_n]

    def t_copy(h, step):
        return pltpu.make_async_remote_copy(
            src_ref=zpart.at[h, step], dst_ref=zback.at[h, step],
            send_sem=t_send.at[h, step], recv_sem=t_recv.at[h, step],
            device_id=(me_n, local_at(step)), device_id_type=MESH,
        )

    @pl.loop(0, parts)
    def _(h):
        @pl.loop(1, n_node)
        def _(step):
            r_copy(h, step).wait_recv()

        def gathered(source):
            spread = xz[source, :, pl.ds(width + exp_w, place_w)][:, :slots]
            found = back[h, source].astype(F32).reshape(slots, part_w).astype(BF16)
            return jnp.dot(spread, found, preferred_element_type=F32).astype(BF16)

        @pl.loop(1, n_local)
        def _(step):
            zpart[h, step] = gathered(local_at(step))
            t_copy(h, step).start()

        zback[h, 0] = gathered(me_l)

    for h in range(parts):
        @pl.loop(1, n_local)
        def _(step):
            t_copy(h, step).wait_recv()

        out_ref[:, pl.ds(h * part_w, part_w)] = jnp.sum(zback[h].astype(F32), axis=0).astype(BF16)

    @pl.loop(1, n_local)
    def _(step):
        z_copy(step).wait_send()

    @pl.loop(0, n_local)
    def _(source):
        @pl.loop(1, n_node)
        def _(step):
            n_copy(source, step).wait_send()

    @pl.loop(0, parts)
    def _(h):
        @pl.loop(1, n_node)
        def _(step):
            r_copy(h, step).wait_send()

        @pl.loop(1, n_local)
        def _(step):
            t_copy(h, step).wait_send()


def shards(quantized, scales, expert_ids, node_choice, gate_weights, w_gate, w_up, w_down):
    n_node = lax.axis_size("node")
    n_local = lax.axis_size("local")
    tok, width = quantized.shape
    ff = w_gate.shape[2]
    cap = node_choice.shape[1] * tok // n_node
    slots = n_node * cap
    total = n_local * slots
    parts = 4
    part_w = width // parts
    exp_w = round_up(n_node * n_local, LANES)
    place_w = round_up(slots, LANES)
    dma = pltpu.SemaphoreType.DMA
    vmem = pl.BlockSpec(memory_space=pltpu.VMEM)
    return pl.pallas_call(
        functools.partial(kernel, n_node, n_local, cap, parts),
        out_shape=jax.ShapeDtypeStruct((tok, width), BF16),
        in_specs=[vmem] * 5 + [pl.BlockSpec(memory_space=pl.ANY)] * 3,
        out_specs=vmem,
        scratch_shapes=[
            pltpu.VMEM((width, ff), BF16),
            pltpu.VMEM((width, ff), BF16),
            pltpu.VMEM((ff, width), BF16),
            pltpu.VMEM((n_local, tok, width + exp_w + place_w), BF16),
            pltpu.VMEM((n_local, n_node, cap, width + exp_w), BF16),
            pltpu.VMEM((n_local, n_node, cap, width + exp_w), BF16),
            pltpu.VMEM((total, width), BF16),
            pltpu.VMEM((total, ff), BF16),
            pltpu.VMEM((parts, n_local, n_node, cap, part_w), BF16),
            pltpu.VMEM((parts, n_local, n_node, cap, part_w), BF16),
            pltpu.VMEM((parts, n_local, tok, part_w), BF16),
            pltpu.VMEM((parts, n_local, tok, part_w), BF16),
            dma((3,)),
            dma((n_local,)), dma((n_local,)),
            dma((n_local, n_node)), dma((n_local, n_node)),
            dma((parts, n_node)), dma((parts, n_node)),
            dma((parts, n_local)), dma((parts, n_local)),
        ],
        compiler_params=pltpu.CompilerParams(
            collective_id=0, has_side_effects=True, vmem_limit_bytes=60 * 1024 * 1024
        ),
    )(
        quantized, scales, expert_ids, node_choice, gate_weights, w_gate[0], w_up[0], w_down[0]
    )


def solution(mesh):
    rows = P(("node", "local"), None)
    mats = P(("node", "local"), None, None)
    return jax.shard_map(
        shards,
        mesh=mesh,
        in_specs=(rows,) * 5 + (mats,) * 3,
        out_specs=rows,
        check_vma=False,
    )
```

time: 138 us -> 69.1 us (0.50)
  waiting for transfers between devices: 90.2 us -> 0 us
  Pallas kernels: 0 us -> 63 us
  matrix products: 19.2 us -> 0 us
  starting transfers between devices: 13.4 us -> 0 us
  other arithmetic: 4.84 us -> 0 us
  local copies, waits for them, and re-layouts: 10.2 us -> 5.6 us
    all_to_all x3 -> x0, waiting for transfers between devices: 90.2 us -> none  [the longest x1 42.9 us: shards(): lax.all_to_all(send_quant, ('node', 'local'), split_axis=0, concat_axis=0...]
    pallas_call x0 -> x1, Pallas kernels: none -> 63 us  [shards(): pl.pallas_call(functools.partial(kernel, n_node, n_local, cap, parts), ou...]
    dot_general x5 -> x0, matrix products: 19.2 us -> none  [the longest x1 10.5 us: expert_apply(): jnp.dot(hidden, down_proj, preferred_element_type=jnp.float32)]
    all_to_all x3 -> x0, starting transfers between devices: 13.4 us -> none  [the longest x1 7.1 us: shards(): lax.all_to_all(send_scale, ('node', 'local'), split_axis=0, concat_axis=0...]
    convert_element_type x4 -> x0, local copies, waits for them, and re-layouts: 6.32 us -> none  [the longest x1 3.1 us: expert_apply(): inputs = widened.reshape(row_count, -1).astype(jnp.bfloat16)]
    unnamed x12 -> x4, local copies, waits for them, and re-layouts: 0.9 us -> 5.6 us
    convert_element_type x3 -> x0, other arithmetic: 3.86 us -> none  [the longest x1 3.84 us: expert_apply(): inputs = widened.reshape(row_count, -1).astype(jnp.bfloat16)]
    gather x6 -> x0, local copies, waits for them, and re-layouts: 2.69 us -> none  [the longest x5 1.58 us: shards(): slot_index = jnp.take_along_axis(earlier, expert_ids, axis=1)]
  transfers between devices with their start and end apart: 3 -> 0, of which waited for: 3 -> 0; matrix products, arithmetic and copies ran while one was open for 2% -> 0% of each run, Pallas kernels for 0% -> 0%
where the time goes in v1:
time: 69.1 us; the launch traced here: 68.6 us
  Pallas kernels  63 us (91%)
  local copies, waits for them, and re-layouts  5.6 us (8%)
    pallas_call x1, Pallas kernels, shards(): pl.pallas_call(functools.partial(kernel, n_node, n_local, cap, parts), ou...  63 us
    unnamed x4, local copies, waits for them, and re-layouts  5.6 us

profile of v1, /device:TPU:1, one launch (start us, length us, event | category | flops | bytes accessed | tf_op | source)
XLA Modules:
  0.0 68.6 jit_solution(16800629670810190913)
XLA Ops:
  0.0 1.3 %copy.11.gate_ref = bf16[16,8]{1,0:T(8,128)(2,1)} copy(bf16[16,8]{0,1:T(8,128)(2,1)} %param.12) | data formatting | bytes 512 | tf_op args[4]
  1.3 1.4 %copy.9.ids_ref = s32[16,8]{1,0:T(8,128)} copy(s32[16,8]{0,1:T(8,128)} %param.10) | data formatting | bytes 1024 | tf_op args[2]
  2.7 1.4 %copy.10.choice_ref = s32[16,4]{1,0:T(8,128)} copy(s32[16,4]{0,1:T(4,128)} %param.11) | data formatting | bytes 512 | tf_op args[3]
  4.1 63.0 %shard_map.82 = bf16[16,3584]{1,0:T(8,128)(2,1)} custom-call(bf16[16,3584]{1,0:T(8,128)(2,1)} %q_ref.1, bf16[16,28]{1,0:T(8,128)(2,1)} %scale_ref.1, s32[16,8]{1,0:T(8,128)} %copy.9.ids_ref, s32[16,4]{1,0:T(8,128)} %copy.10.choice_ref, bf16[16,8]{1,0:T(8,128)(2,1)} %copy.11.gate_ref, bf16[3584,1024]{1,0:T(8,128)(2,1)} %bitcast.3, ...), custom_call_target="tpu_custom_call" | custom-call | tf_op jit(solution)/shard_map/pallas_call | solution.py:227
  67.0 1.6 %copy.13 = bf16[16,3584]{1,0:T(8,128)(2,1)} copy(bf16[16,3584]{1,0:T(8,128)(2,1)} %shard_map.82) | data formatting | bytes 229376
